TPU v7x, 512 devices: a whole 4x4x16 slice. The times are simulated.
512 devices in a mesh: dp: 32 (over z, core), tensor: 16 (over y, x).
Axes of the slice: x: 4, y: 4, z: 16, core: 2. Of those that a mesh axis runs over, the one named last changes fastest.
Arguments:
- grads: bfloat16 [32, 2048, 5632], P('dp', None, 'tensor'), may hold values from -6 to 6
- errors: bfloat16 [32, 2048, 5632], P('dp', None, 'tensor'), may hold values from -4 to 4
- q_start: float32 [5632, 32], P('tensor'), may hold values from -6 to 6
Outputs:
- new_errors: bfloat16 [32, 2048, 5632], P('dp', None, 'tensor')
- p_hat: float32 [2048, 32], replicated
- q_new: float32 [5632, 32], P('tensor')
All inputs are finite; a program needn't handle non-finite values.
Results may differ from a plain program's by a relative error of at most 0.012.
Values sent between devices are 32-bit elements; how exact they have to be, the bound alone decides.
A program may use at most 64 MiB of HBM per device.

v0:
```python
import jax
import jax.numpy as jnp
from jax import lax
from jax.sharding import PartitionSpec as P


def solve_right(lower_factor, values):
    return lax.linalg.triangular_solve(
        lower_factor, values, left_side=False, lower=True, transpose_a=True
    )


def body(grads, errors, q_start):
    merged = (grads[0].astype(jnp.float32) + errors[0].astype(jnp.float32)).astype(jnp.bfloat16)
    q_narrow = q_start.astype(jnp.bfloat16)
    p_part = jnp.dot(merged, q_narrow, preferred_element_type=jnp.float32)
    p_sum = lax.psum(p_part, ("dp", "tensor"))
    gram_matrix = jnp.dot(p_sum.T, p_sum, precision=lax.Precision.HIGHEST)
    lower_factor = jnp.linalg.cholesky(gram_matrix)
    p_hat = solve_right(lower_factor, p_sum)
    p_narrow = p_hat.astype(jnp.bfloat16)
    q_part = lax.dot_general(
        merged, p_narrow, (((0,), (0,)), ((), ())), preferred_element_type=jnp.float32
    )
    q_new = lax.psum(q_part, "dp") / lax.axis_size("dp")
    delta = jnp.dot(p_hat, q_new.T, precision=lax.Precision.HIGHEST)
    new_errors = (merged.astype(jnp.float32) - delta).astype(jnp.bfloat16)[None]
    return (new_errors, p_hat, q_new)


def solution(mesh):
    placed = (P("dp", None, "tensor"), P("dp", None, "tensor"), P("tensor", None))
    return jax.shard_map(
        body,
        mesh=mesh,
        in_specs=placed,
        out_specs=(P("dp", None, "tensor"), P(), P("tensor", None)),
        check_vma=False,
    )
```

profile of v0, /device:TPU:1, one launch (start us, length us, event | category | flops | bytes accessed | tf_op | source)
XLA Modules:
  0.0 584.6 jit_solution(17089700179756453151)
XLA Ops:
  7.2 0.0 all-reduce.2.cloned.1.call-start
  7.2 0.0 copy-start.1
  7.2 3.1 fusion.5
  10.4 0.0 copy-start
  10.4 0.0 all-reduce.2.cloned.1.call-update
  10.4 464.1 %all-reduce.2.cloned.1.call-done = f32[2048,32]{0,1:T(8,128)} async-done(((f32[2048,32]{0,1:T(8,128)}), f32[2048,32]{0,1:T(8,128)}) %all-reduce.2.cloned.1.call-update) | async-done | bytes 262160 | tf_op jit(solution)/shard_map/psum | solution.py:17
  474.5 1.4 fusion.13
  475.9 0.1 copy.6
  476.0 2.9 cholesky.16
  478.9 0.6 compare_reduce_fusion
  479.6 0.7 fusion.7
  480.2 2.4 custom-call.6
  482.7 1.4 fusion.8
  484.1 0.0 copy-done.1
  484.1 0.0 copy-done
  484.1 0.0 copy-start.2
  484.1 0.5 fusion.3
  484.6 89.4 %psum.15 = f32[352,32]{0,1:T(8,128)S(1)} all-reduce(f32[352,32]{0,1:T(8,128)S(1)} %fusion.3), channel_id=1, replica_groups=mesh['dp'=32,'tensor'=16] {'dp'}, use_global_device_ids=true, to_apply=%region_3.4 | all-reduce | flops 11264 | bytes 90112 | tf_op jit(solution)/shard_map/psum | solution.py:25
  574.0 0.0 copy-done.2
  574.0 0.0 copy-start.3
  574.0 3.7 fusion.1
  577.7 0.0 copy-done.3
  (3 shorter events, 0.0 us)
Async XLA Ops:
  7.2 467.3 %all-reduce.2.cloned.1.call-start = ((), (), s32[]{:S(2)}) async-start(), calls=%async_computation | async-start | bytes 524288 | tf_op jit(solution)/shard_map/psum | solution.py:17
  7.2 476.8 %copy-start.1 = (bf16[1,2048,352]{1,2,0:T(8,128)(2,1)S(1)}, bf16[1,2048,352]{1,2,0:T(8,128)(2,1)}, u32[]{:S(2)}) copy-start(bf16[1,2048,352]{1,2,0:T(8,128)(2,1)} %param.3) | copy-start | bytes 4325380
  10.4 473.7 %copy-start = (bf16[1,2048,352]{1,2,0:T(8,128)(2,1)S(1)}, bf16[1,2048,352]{1,2,0:T(8,128)(2,1)}, u32[]{:S(2)}) copy-start(bf16[1,2048,352]{1,2,0:T(8,128)(2,1)} %param.4) | copy-start | bytes 4325380
  484.1 90.0 %copy-start.2 = (f32[2048,32]{0,1:T(8,128)}, f32[2048,32]{0,1:T(8,128)S(1)}, u32[]{:S(2)}) copy-start(f32[2048,32]{0,1:T(8,128)S(1)} %fusion.8) | copy-start | bytes 786436
  574.0 3.7 copy-start.3
Sparse Core Ops, SparseCore 0:
  14.0 460.4 all-reduce.1
where the time goes:
time: 587 us; the launch traced here: 585 us
  waiting for transfers between devices  464 us (79%)
  blocking collectives  89.4 us (15%)
  between operations  14.1 us (2%)
  matrix products  10.1 us (2%)
  other arithmetic  6.7 us (1%)
    psum x1, waiting for transfers between devices, body(): p_sum = lax.psum(p_part, ('dp', 'tensor'))  464 us
    psum x1, blocking collectives, body(): q_new = lax.psum(q_part, 'dp') / lax.axis_size('dp')  89.4 us
  transfers between devices with their start and end apart: 1, of which 1 were waited for; matrix products, arithmetic and copies ran while one was open for 0% of the time, Pallas kernels for 0%

commit v1 on v0

v1 whole, which is shorter than its diff:
```python
import functools

import jax
import jax.numpy as jnp
from jax import lax
from jax.experimental import pallas as pl
from jax.experimental.pallas import tpu as pltpu
from jax.sharding import PartitionSpec as P

MESH = pl.DeviceIdType.MESH
HIGHEST = lax.Precision.HIGHEST
F32, BF16 = jnp.float32, jnp.bfloat16

RANK = 32
ROWS = 2048
COLS = 352
WIDE = 384
STEP = 256
STEPS = ROWS // STEP

FAR = {0: 0, 1: 1, 2: 2, 3: 1}
OFFSETS = sorted(
    ((j, y, x) for j in range(2) for y in range(4) for x in range(4) if (j, y, x) != (0, 0, 0)),
    key=lambda o: -(o[0] + FAR[o[1]] + FAR[o[2]]),
)
GROUPS = [4, 3, 5, 2, 6, 1, 7]


def split3(value):
    hi = value.astype(BF16)
    rest = value - hi.astype(F32)
    mid = rest.astype(BF16)
    lo = (rest - mid.astype(F32)).astype(BF16)
    return hi, mid, lo


def kernel(
    grads, errors, q_start, merged_out, p_split, p_out, q_out,
    q_in, gbuf, ebuf, parts_buf, pt, core_rx, a_src, a_rx, b_src, b_rx, p_full,
    q_part, d_rx, e_src, e_rx, q_full,
    q_sem, load_sem, core_send, core_recv, a_send, a_recv, b_send, b_recv, c_send, c_recv,
    f_send, f_recv, d_send, d_recv, e_send, e_recv, g_send, g_recv,
):
    dp, tensor = lax.axis_index("dp"), lax.axis_index("tensor")
    z, core = dp // 2, dp % 2
    group, bit = z // 2, z % 2
    member = (bit + group // 4) % 2
    y, x = tensor // 4, tensor % 4

    def chip(a, j):
        return 2 * a + (j + a // 4) % 2

    def plane_peer(o):
        j, py, px = (member + o[0]) % 2, (y + o[1]) % 4, (x + o[2]) % 4
        t = py * 4 + px
        return (chip(group, j) * 2 + core, t), j * 16 + t

    def group_peer(k):
        a = (group + k) % 8
        return (chip(a, member) * 2 + core, tensor)

    sibling = (z * 2 + 1 - core, tensor)
    across = (chip(group, 1 - member) * 2 + 1 - core, tensor)
    beside = (chip(group, 1 - member) * 2 + core, tensor)
    mine = member * 16 + tensor

    def cols(i):
        return pl.ds(pl.multiple_of(i * STEP, STEP), STEP)

    def load(i):
        at = ((1 - core) * (STEPS // 2) + i) % STEPS
        return (
            pltpu.make_async_copy(grads.at[:, cols(at)], gbuf.at[:, cols(at)], load_sem.at[0, i]),
            pltpu.make_async_copy(errors.at[:, cols(at)], ebuf.at[:, cols(at)], load_sem.at[1, i]),
        )

    q_copy = pltpu.make_async_copy(q_start, q_in, q_sem)
    q_copy.start()
    for i in range(STEPS):
        for copy in load(i):
            copy.start()

    barrier = pltpu.get_barrier_semaphore()
    for k in GROUPS:
        pl.semaphore_signal(barrier, inc=1, device_id=group_peer(k), device_id_type=MESH)
    for o in OFFSETS:
        pl.semaphore_signal(barrier, inc=1, device_id=plane_peer(o)[0], device_id_type=MESH)
    pl.semaphore_signal(barrier, inc=1, device_id=across, device_id_type=MESH)
    pl.semaphore_signal(barrier, inc=1, device_id=sibling, device_id_type=MESH)

    q_copy.wait()
    q_narrow = q_in[...].astype(BF16)

    def left(i):
        for copy in load(i):
            copy.wait()
        at = ((1 - core) * (STEPS // 2) + i) % STEPS
        merged = (gbuf[:, cols(at)].astype(F32) + ebuf[:, cols(at)].astype(F32)).astype(BF16)
        merged_out[:, cols(at)] = merged
        part = jnp.dot(q_narrow, merged, preferred_element_type=F32)
        for h in range(2):
            pt[pl.ds(at * 8 + h * 4, 4)] = part[:, h * 128 : (h + 1) * 128].reshape(4, 8, 128)

    for i in range(STEPS // 2):
        left(i)
    pl.semaphore_wait(barrier, len(GROUPS) + len(OFFSETS) + 2)
    core_copy = pltpu.make_async_remote_copy(
        src_ref=pt.at[pl.ds((1 - core) * 32, 32)], dst_ref=core_rx,
        send_sem=core_send, recv_sem=core_recv, device_id=sibling, device_id_type=MESH,
    )
    core_copy.start()
    for i in range(STEPS // 2, STEPS):
        left(i)
    core_copy.wait_recv()
    a_src[...] = pt[pl.ds(core * 32, 32)] + core_rx[...]

    for n, o in enumerate(OFFSETS):
        device, chunk = plane_peer(o)
        pltpu.make_async_remote_copy(
            src_ref=a_src.at[chunk], dst_ref=a_rx.at[n],
            send_sem=a_send, recv_sem=a_recv, device_id=device, device_id_type=MESH,
        ).start()

    def all_of(ref, send, recv):
        return pltpu.make_async_remote_copy(
            src_ref=ref, dst_ref=ref, send_sem=send, recv_sem=recv, device_id=sibling, device_id_type=MESH
        )

    all_a = all_of(a_rx, a_send, a_recv)
    all_a.wait_recv()
    total = a_src[mine]
    for n in range(len(OFFSETS)):
        total = total + a_rx[n]
    b_src[...] = total
    b_rx[group] = total

    for k in GROUPS:
        pltpu.make_async_remote_copy(
            src_ref=b_src, dst_ref=b_rx.at[group],
            send_sem=b_send, recv_sem=b_recv, device_id=group_peer(k), device_id_type=MESH,
        ).start()
    all_b = all_of(b_rx.at[pl.ds(0, 7)], b_send, b_recv)
    all_b.wait_recv()
    total = b_rx[0]
    for k in range(1, 8):
        total = total + b_rx[k]
    p_full[core * 32 + mine] = total

    for n, o in enumerate(OFFSETS):
        pltpu.make_async_remote_copy(
            src_ref=p_full.at[core * 32 + mine], dst_ref=p_full.at[core * 32 + mine],
            send_sem=c_send, recv_sem=c_recv, device_id=plane_peer(o)[0], device_id_type=MESH,
        ).start()
    all_c = all_of(p_full.at[pl.ds(0, 31)], c_send, c_recv)
    all_c.wait_recv()
    half = pl.ds(core * 32, 32)
    half_copy = pltpu.make_async_remote_copy(
        src_ref=p_full.at[half], dst_ref=p_full.at[half],
        send_sem=f_send, recv_sem=f_recv, device_id=sibling, device_id_type=MESH,
    )
    half_copy.start()

    def right(at):
        tiles = [p_full[pl.ds(at * 8 + h * 4, 4)].reshape(RANK, 128) for h in range(2)]
        parts = jnp.concatenate(split3(jnp.concatenate(tiles, axis=1)), axis=0)
        parts_buf[:, cols(at)] = parts
        return lax.dot_general(
            parts, merged_out[:, cols(at)], (((1,), (1,)), ((), ())), preferred_element_type=F32
        )

    def right_half(c):
        acc = right(c * (STEPS // 2))
        for i in range(1, STEPS // 2):
            acc = acc + right(c * (STEPS // 2) + i)
        return acc

    acc = right_half(core)
    half_copy.wait_recv()
    acc = acc + right_half(1 - core)
    acc = acc[2 * RANK :] + acc[RANK : 2 * RANK] + acc[0:RANK]
    q_part[:, :, 0:COLS] = acc.reshape(4, 8, COLS)
    q_part[:, :, COLS:] = jnp.zeros((4, 8, WIDE - COLS), F32)

    def owner(j, c):
        return j * 2 + c

    me = owner(member, core)
    partners = (
        (across, owner(1 - member, 1 - core)),
        (beside, owner(1 - member, core)),
        (sibling, owner(member, 1 - core)),
    )
    for n, (device, chunk) in enumerate(partners):
        pltpu.make_async_remote_copy(
            src_ref=q_part.at[chunk], dst_ref=d_rx.at[n],
            send_sem=d_send, recv_sem=d_recv, device_id=device, device_id_type=MESH,
        ).start()
    gram = lax.dot_general(
        parts_buf[...], parts_buf[...], (((1,), (1,)), ((), ())), preferred_element_type=F32
    )
    gram = gram[2 * RANK :] + gram[RANK : 2 * RANK] + gram[0:RANK]
    gram = gram[:, 2 * RANK :] + gram[:, RANK : 2 * RANK] + gram[:, 0:RANK]
    all_d = all_of(d_rx, d_send, d_recv)
    all_d.wait_recv()
    total = q_part[me] + d_rx[0] + d_rx[1] + d_rx[2]
    e_src[...] = total
    e_rx[group] = total
    for k in GROUPS:
        pltpu.make_async_remote_copy(
            src_ref=e_src, dst_ref=e_rx.at[group],
            send_sem=e_send, recv_sem=e_recv, device_id=group_peer(k), device_id_type=MESH,
        ).start()

    row = lax.broadcasted_iota(jnp.int32, (RANK, 2 * RANK), 0)
    col = lax.broadcasted_iota(jnp.int32, (RANK, 2 * RANK), 1)
    unit = jnp.where(col == row + RANK, 1.0, 0.0).astype(F32)
    work = jnp.concatenate([gram, unit[:, RANK:]], axis=1)
    below = lax.broadcasted_iota(jnp.int32, (RANK, 1), 0)
    for k in range(RANK - 1):
        pivot = work[k : k + 1, :]
        factor = work[:, k : k + 1] / work[k : k + 1, k : k + 1]
        work = work - jnp.where(below > k, factor, 0.0) * pivot
    diagonal = jnp.sum(jnp.where(row == col, work, 0.0), axis=1, keepdims=True)
    inverse = work[:, RANK:] / jnp.sqrt(diagonal)

    for i in range(STEPS):
        tiles = [p_full[pl.ds(i * 8 + h * 4, 4)].reshape(RANK, 128) for h in range(2)]
        p_hat = jnp.dot(inverse, jnp.concatenate(tiles, axis=1), precision=HIGHEST, preferred_element_type=F32)
        p_out[:, cols(i)] = p_hat
        hi, mid, lo = split3(p_hat)
        p_split[:, cols(i)] = jnp.concatenate([hi, mid, hi, mid, lo, hi], axis=0)

    all_e = all_of(e_rx.at[pl.ds(0, 7)], e_send, e_recv)
    all_e.wait_recv()
    total = e_rx[0]
    for k in range(1, 8):
        total = total + e_rx[k]
    q_full[me] = total
    for n, (device, _) in enumerate(partners):
        pltpu.make_async_remote_copy(
            src_ref=q_full.at[me], dst_ref=q_full.at[me],
            send_sem=g_send, recv_sem=g_recv, device_id=device, device_id_type=MESH,
        ).start()
    all_g = all_of(q_full.at[pl.ds(0, 3)], g_send, g_recv)
    all_g.wait_recv()
    q_sum = q_full[...].reshape(RANK, WIDE)
    q_new = jnp.dot(inverse, q_sum, precision=HIGHEST, preferred_element_type=F32) * (1.0 / 32.0)
    q_out[...] = q_new[:, 0:COLS]
    core_copy.wait_send()
    all_a.wait_send()
    all_b.wait_send()
    all_c.wait_send()
    half_copy.wait_send()
    all_d.wait_send()
    all_e.wait_send()
    all_g.wait_send()


def update_kernel(merged, p_split, p_hat, q_new, new_errors, p_out, q_out, stage, out_sem, side_sem):
    p_copy = pltpu.make_async_copy(p_hat, p_out, side_sem.at[0])
    q_copy = pltpu.make_async_copy(q_new, q_out, side_sem.at[1])
    p_copy.start()
    q_copy.start()
    hi, mid, lo = split3(q_new[...].T)
    q_split = jnp.concatenate([hi, hi, mid, mid, hi, lo], axis=1)

    def store(i):
        at = pl.ds(i * STEP, STEP)
        return pltpu.make_async_copy(stage.at[:, at], new_errors.at[:, at], out_sem.at[i])

    for i in range(STEPS):
        at = pl.ds(i * STEP, STEP)
        delta = jnp.dot(q_split, p_split[:, at], preferred_element_type=F32)
        stage[:, at] = (merged[:, at].astype(F32) - delta).astype(BF16)
        store(i).start()
    p_copy.wait()
    q_copy.wait()
    for i in range(STEPS):
        store(i).wait()


def body(grads, errors, q_start):
    hbm_spec = pl.BlockSpec(memory_space=pltpu.HBM)
    vmem_spec = pl.BlockSpec(memory_space=pltpu.VMEM)
    dma = pltpu.SemaphoreType.DMA
    tile = (8, 128)
    strip = (8, WIDE)
    merged, p_split, p_hat, q_new = pl.pallas_call(
        kernel,
        name="factors",
        out_shape=(
            jax.ShapeDtypeStruct((COLS, ROWS), BF16),
            jax.ShapeDtypeStruct((6 * RANK, ROWS), BF16),
            jax.ShapeDtypeStruct((RANK, ROWS), F32),
            jax.ShapeDtypeStruct((RANK, COLS), F32),
        ),
        in_specs=[hbm_spec, hbm_spec, hbm_spec],
        out_specs=(vmem_spec,) * 4,
        scratch_shapes=[
            pltpu.VMEM((RANK, COLS), F32),
            pltpu.VMEM((COLS, ROWS), BF16),
            pltpu.VMEM((COLS, ROWS), BF16),
            pltpu.VMEM((3 * RANK, ROWS), BF16),
            pltpu.VMEM((64,) + tile, F32),
            pltpu.VMEM((32,) + tile, F32),
            pltpu.VMEM((32,) + tile, F32),
            pltpu.VMEM((31,) + tile, F32),
            pltpu.VMEM(tile, F32),
            pltpu.VMEM((8,) + tile, F32),
            pltpu.VMEM((64,) + tile, F32),
            pltpu.VMEM((4,) + strip, F32),
            pltpu.VMEM((3,) + strip, F32),
            pltpu.VMEM(strip, F32),
            pltpu.VMEM((8,) + strip, F32),
            pltpu.VMEM((4,) + strip, F32),
            dma,
            dma((2, STEPS)),
        ]
        + [dma] * 16,
        compiler_params=pltpu.CompilerParams(
            collective_id=0, has_side_effects=True, vmem_limit_bytes=32 * 1024 * 1024
        ),
    )(*(pltpu.with_memory_space_constraint(a, pltpu.HBM) for a in (grads[0].T, errors[0].T, q_start.T)))
    new_errors, p_hat, q_new = pl.pallas_call(
        update_kernel,
        name="update",
        out_shape=(
            jax.ShapeDtypeStruct((COLS, ROWS), BF16),
            jax.ShapeDtypeStruct((RANK, ROWS), F32),
            jax.ShapeDtypeStruct((RANK, COLS), F32),
        ),
        in_specs=[vmem_spec] * 4,
        out_specs=(hbm_spec,) * 3,
        scratch_shapes=[pltpu.VMEM((COLS, ROWS), BF16), dma((STEPS,)), dma((2,))],
        compiler_params=pltpu.CompilerParams(vmem_limit_bytes=16 * 1024 * 1024),
    )(merged, p_split, p_hat, q_new)
    return new_errors.T[None], p_hat.T, q_new.T


def solution(mesh):
    placed = (P("dp", None, "tensor"), P("dp", None, "tensor"), P("tensor", None))
    return jax.shard_map(
        body,
        mesh=mesh,
        in_specs=placed,
        out_specs=(P("dp", None, "tensor"), P(), P("tensor", None)),
        check_vma=False,
    )
```

time: 587 us -> 55 us (0.09)
  waiting for transfers between devices: 464 us -> 0 us
  blocking collectives: 89.4 us -> 0 us
  Pallas kernels: 0 us -> 54.2 us
  between operations: 14.1 us -> 0.64 us
  matrix products: 10.1 us -> 0 us
  other arithmetic: 6.7 us -> 0 us
    psum x1 -> x0, waiting for transfers between devices: 464 us -> none  [body(): p_sum = lax.psum(p_part, ('dp', 'tensor'))]
    psum x1 -> x0, blocking collectives: 89.4 us -> none  [body(): q_new = lax.psum(q_part, 'dp') / lax.axis_size('dp')]
    pallas_call x0 -> x2, Pallas kernels: none -> 54.2 us  [the longest x1 52.4 us: body(): pl.pallas_call(kernel, name='factors', out_shape=(jax.ShapeDtypeStruct((C...]
    dot_general x4 -> x0, matrix products: 8.72 us -> none  [the longest x1 3.7 us: body(): delta = jnp.dot(p_hat, q_new.T, precision=lax.Precision.HIGHEST)]
    another operation x5 -> x0, other arithmetic: 6.68 us -> none  [the longest x3 3.6 us: body(): lower_factor = jnp.linalg.cholesky(gram_matrix)]
  transfers between devices with their start and end apart: 1 -> 0, of which waited for: 1 -> 0; matrix products, arithmetic and copies ran while one was open for 0% -> 0% of each run, Pallas kernels for 0% -> 0%
where the time goes in v1:
time: 55 us; the launch traced here: 54.8 us
  Pallas kernels  54.2 us (99%)
  between operations  0.64 us (1%)
    pallas_call x1, Pallas kernels, body(): pl.pallas_call(kernel, name='factors', out_shape=(jax.ShapeDtypeStruct((C...  52.4 us
    pallas_call x1, Pallas kernels, body(): pl.pallas_call(update_kernel, name='update', out_shape=(jax.ShapeDtypeStr...  1.78 us

profile of v1, /device:TPU:1, one launch (start us, length us, event | category | flops | bytes accessed | tf_op | source)
XLA Modules:
  0.0 54.8 jit_solution(2826454553998403031)
XLA Ops:
  0.6 52.4 %factors.1 = (bf16[352,2048]{1,0:T(8,128)(2,1)S(1)}, bf16[192,2048]{1,0:T(8,128)(2,1)S(1)}, f32[32,2048]{1,0:T(8,128)S(1)}, f32[32,352]{1,0:T(8,128)S(1)}) custom-call(bf16[352,2048]{1,0:T(8,128)(2,1)} %bitcast.12, bf16[352,2048]{1,0:T(8,128)(2,1)} %bitcast.13, f32[32,352]{1,0:T(8,128)} %bitcast.14), custom_call_target="tpu_custom_call" | custom-call | tf_op jit(solution)/shard_map/factors/pallas_call | solution.py:288
  53.1 1.8 %update.1 = (bf16[352,2048]{1,0:T(8,128)(2,1)}, f32[32,2048]{1,0:T(8,128)}, f32[32,352]{1,0:T(8,128)}) custom-call(bf16[352,2048]{1,0:T(8,128)(2,1)S(1)} %get-tuple-element.10.merged, bf16[192,2048]{1,0:T(8,128)(2,1)S(1)} %get-tuple-element.11.p_split, f32[32,2048]{1,0:T(8,128)S(1)} %get-tuple-element.12.p_hat, f32[32,352]{1,0:T(8,128)S(1)} %get-tuple-element.13.q_new), custom_call_target="tpu_custom_call" | custom-call | tf_op jit(solution)/shard_map/update/pallas_call | solution.py:324

commit v2 on v1

--- a/solution.py
+++ b/solution.py
@@ -37,38 +37,45 @@
 def kernel(
     grads, errors, q_start, merged_out, p_split, p_out, q_out,
     q_in, gbuf, ebuf, parts_buf, pt, core_rx, a_src, a_rx, b_src, b_rx, p_full,
-    q_part, d_rx, e_src, e_rx, q_full,
-    q_sem, load_sem, core_send, core_recv, a_send, a_recv, b_send, b_recv, c_send, c_recv,
+    q_part, d_rx, e_src, e_rx, q_full, m_src, m_rx, m_hi, m_lo,
+    ready, m_send, m_recv, q_sem, load_sem, core_send, core_recv, a_send, a_recv, b_send, b_recv, c_send, c_recv,
     f_send, f_recv, d_send, d_recv, e_send, e_recv, g_send, g_recv,
 ):
     dp, tensor = lax.axis_index("dp"), lax.axis_index("tensor")
-    z, core = dp // 2, dp % 2
-    group, bit = z // 2, z % 2
-    member = (bit + group // 4) % 2
-    y, x = tensor // 4, tensor % 4
-
-    def chip(a, j):
-        return 2 * a + (j + a // 4) % 2
+    z, core = lax.div(dp, 2), lax.rem(dp, 2)
+    group, bit = lax.div(z, 2), lax.rem(z, 2)
+    member = lax.rem(bit + lax.div(group, 4), 2)
+    y, x = lax.div(tensor, 4), lax.rem(tensor, 4)
+    columns_of = [lax.rem(x + k, 4) for k in range(4)]
+    rows_of = [lax.rem(y + k, 4) * 4 for k in range(4)]
+    members = [member, 1 - member]
+    in_pair = [dp, 4 * group + 2 * (1 - bit) + core]
 
     def plane_peer(o):
-        j, py, px = (member + o[0]) % 2, (y + o[1]) % 4, (x + o[2]) % 4
-        t = py * 4 + px
-        return (chip(group, j) * 2 + core, t), j * 16 + t
+        t = rows_of[o[1]] + columns_of[o[2]]
+        return (in_pair[o[0]], t), members[o[0]] * 16 + t
+
+    def group_at(a):
+        return (4 * a + 2 * (member if a < 4 else 1 - member) + core, tensor)
 
     def group_peer(k):
-        a = (group + k) % 8
-        return (chip(a, member) * 2 + core, tensor)
-
-    sibling = (z * 2 + 1 - core, tensor)
-    across = (chip(group, 1 - member) * 2 + 1 - core, tensor)
-    beside = (chip(group, 1 - member) * 2 + core, tensor)
+        a = lax.rem(group + k, 8)
+        return (4 * a + 2 * lax.rem(member + lax.div(a, 4), 2) + core, tensor)
+
+    other = 1 - core
+    sibling = (dp + other - core, tensor)
+    beside = (in_pair[1], tensor)
+    across = (in_pair[1] + other - core, tensor)
     mine = member * 16 + tensor
 
     def cols(i):
         return pl.ds(pl.multiple_of(i * STEP, STEP), STEP)
 
+    def half_at(i):
+        return (other if i < STEPS // 2 else core) * (STEPS // 2) + i % (STEPS // 2)
+
     def load(i):
-        at = ((1 - core) * (STEPS // 2) + i) % STEPS
+        at = half_at(i)
         return (
             pltpu.make_async_copy(grads.at[:, cols(at)], gbuf.at[:, cols(at)], load_sem.at[0, i]),
             pltpu.make_async_copy(errors.at[:, cols(at)], ebuf.at[:, cols(at)], load_sem.at[1, i]),
@@ -81,8 +88,12 @@
             copy.start()
 
     barrier = pltpu.get_barrier_semaphore()
-    for k in GROUPS:
-        pl.semaphore_signal(barrier, inc=1, device_id=group_peer(k), device_id_type=MESH)
+    for a in range(8):
+
+        @pl.when(group < a)
+        def _():
+            pl.semaphore_signal(barrier, inc=1, device_id=group_at(a), device_id_type=MESH)
+
     for o in OFFSETS:
         pl.semaphore_signal(barrier, inc=1, device_id=plane_peer(o)[0], device_id_type=MESH)
     pl.semaphore_signal(barrier, inc=1, device_id=across, device_id_type=MESH)
@@ -94,7 +105,7 @@
     def left(i):
         for copy in load(i):
             copy.wait()
-        at = ((1 - core) * (STEPS // 2) + i) % STEPS
+        at = half_at(i)
         merged = (gbuf[:, cols(at)].astype(F32) + ebuf[:, cols(at)].astype(F32)).astype(BF16)
         merged_out[:, cols(at)] = merged
         part = jnp.dot(q_narrow, merged, preferred_element_type=F32)
@@ -103,9 +114,15 @@
 
     for i in range(STEPS // 2):
         left(i)
-    pl.semaphore_wait(barrier, len(GROUPS) + len(OFFSETS) + 2)
+    pl.semaphore_wait(barrier, len(OFFSETS) + 2 + group)
+    for a in range(8):
+
+        @pl.when(group > a)
+        def _():
+            pl.semaphore_signal(ready, inc=1, device_id=group_at(a), device_id_type=MESH)
+
     core_copy = pltpu.make_async_remote_copy(
-        src_ref=pt.at[pl.ds((1 - core) * 32, 32)], dst_ref=core_rx,
+        src_ref=pt.at[pl.ds(other * 32, 32)], dst_ref=core_rx,
         send_sem=core_send, recv_sem=core_recv, device_id=sibling, device_id_type=MESH,
     )
     core_copy.start()
@@ -121,6 +138,17 @@
             send_sem=a_send, recv_sem=a_recv, device_id=device, device_id_type=MESH,
         ).start()
 
+    def swap(i):
+        part = pl.ds(i * STEP, STEP)
+        return pltpu.make_async_remote_copy(
+            src_ref=m_src.at[:, part], dst_ref=m_rx.at[:, part],
+            send_sem=m_send.at[i], recv_sem=m_recv.at[i], device_id=sibling, device_id_type=MESH,
+        )
+
+    for i in range(STEPS // 2):
+        m_src[:, i * STEP : (i + 1) * STEP] = merged_out[:, cols(half_at(i))].astype(F32)
+        swap(i).start()
+
     def all_of(ref, send, recv):
         return pltpu.make_async_remote_copy(
             src_ref=ref, dst_ref=ref, send_sem=send, recv_sem=recv, device_id=sibling, device_id_type=MESH
@@ -134,11 +162,36 @@
     b_src[...] = total
     b_rx[group] = total
 
-    for k in GROUPS:
+    def spread(a):
         pltpu.make_async_remote_copy(
             src_ref=b_src, dst_ref=b_rx.at[group],
-            send_sem=b_send, recv_sem=b_recv, device_id=group_peer(k), device_id_type=MESH,
-        ).start()
+            send_sem=b_send, recv_sem=b_recv, device_id=group_at(a), device_id_type=MESH,
+        ).start()
+
+    for a in range(7):
+
+        @pl.when(group > a)
+        def _():
+            spread(a)
+
+    @pl.when(group < 7)
+    def _():
+        pl.semaphore_wait(ready, 7 - group)
+
+    for a in range(7, 0, -1):
+
+        @pl.when(group < a)
+        def _():
+            spread(a)
+
+    for i in range(STEPS // 2):
+        part = slice(i * STEP, (i + 1) * STEP)
+        swap(i).wait_recv()
+        both = merged_out[:, cols(core * (STEPS // 2) + i)].astype(F32) + m_rx[:, part]
+        hi = both.astype(BF16)
+        m_hi[:, part] = hi
+        m_lo[:, part] = (both - hi.astype(F32)).astype(BF16)
+
     all_b = all_of(b_rx.at[pl.ds(0, 7)], b_send, b_recv)
     all_b.wait_recv()
     total = b_rx[0]
@@ -160,23 +213,19 @@
     )
     half_copy.start()
 
-    def right(at):
+    def left_parts(at):
         tiles = [p_full[pl.ds(at * 8 + h * 4, 4)].reshape(RANK, 128) for h in range(2)]
         parts = jnp.concatenate(split3(jnp.concatenate(tiles, axis=1)), axis=0)
         parts_buf[:, cols(at)] = parts
-        return lax.dot_general(
-            parts, merged_out[:, cols(at)], (((1,), (1,)), ((), ())), preferred_element_type=F32
-        )
-
-    def right_half(c):
-        acc = right(c * (STEPS // 2))
-        for i in range(1, STEPS // 2):
-            acc = acc + right(c * (STEPS // 2) + i)
-        return acc
-
-    acc = right_half(core)
-    half_copy.wait_recv()
-    acc = acc + right_half(1 - core)
+        return parts
+
+    turned = (((1,), (1,)), ((), ()))
+    acc = jnp.zeros((3 * RANK, COLS), F32)
+    for i in range(STEPS // 2):
+        part = slice(i * STEP, (i + 1) * STEP)
+        parts = left_parts(core * (STEPS // 2) + i)
+        acc = acc + lax.dot_general(parts, m_lo[:, part], turned, preferred_element_type=F32)
+        acc = acc + lax.dot_general(parts, m_hi[:, part], turned, preferred_element_type=F32)
     acc = acc[2 * RANK :] + acc[RANK : 2 * RANK] + acc[0:RANK]
     q_part[:, :, 0:COLS] = acc.reshape(4, 8, COLS)
     q_part[:, :, COLS:] = jnp.zeros((4, 8, WIDE - COLS), F32)
@@ -186,20 +235,15 @@
 
     me = owner(member, core)
     partners = (
-        (across, owner(1 - member, 1 - core)),
+        (across, owner(1 - member, other)),
         (beside, owner(1 - member, core)),
-        (sibling, owner(member, 1 - core)),
+        (sibling, owner(member, other)),
     )
     for n, (device, chunk) in enumerate(partners):
         pltpu.make_async_remote_copy(
             src_ref=q_part.at[chunk], dst_ref=d_rx.at[n],
             send_sem=d_send, recv_sem=d_recv, device_id=device, device_id_type=MESH,
         ).start()
-    gram = lax.dot_general(
-        parts_buf[...], parts_buf[...], (((1,), (1,)), ((), ())), preferred_element_type=F32
-    )
-    gram = gram[2 * RANK :] + gram[RANK : 2 * RANK] + gram[0:RANK]
-    gram = gram[:, 2 * RANK :] + gram[:, RANK : 2 * RANK] + gram[:, 0:RANK]
     all_d = all_of(d_rx, d_send, d_recv)
     all_d.wait_recv()
     total = q_part[me] + d_rx[0] + d_rx[1] + d_rx[2]
@@ -210,6 +254,15 @@
             src_ref=e_src, dst_ref=e_rx.at[group],
             send_sem=e_send, recv_sem=e_recv, device_id=group_peer(k), device_id_type=MESH,
         ).start()
+
+    half_copy.wait_recv()
+    for i in range(STEPS // 2):
+        left_parts(other * (STEPS // 2) + i)
+    gram = lax.dot_general(
+        parts_buf[...], parts_buf[...], (((1,), (1,)), ((), ())), preferred_element_type=F32
+    )
+    gram = gram[2 * RANK :] + gram[RANK : 2 * RANK] + gram[0:RANK]
+    gram = gram[:, 2 * RANK :] + gram[:, RANK : 2 * RANK] + gram[:, 0:RANK]
 
     row = lax.broadcasted_iota(jnp.int32, (RANK, 2 * RANK), 0)
     col = lax.broadcasted_iota(jnp.int32, (RANK, 2 * RANK), 1)
@@ -230,6 +283,9 @@
         hi, mid, lo = split3(p_hat)
         p_split[:, cols(i)] = jnp.concatenate([hi, mid, hi, mid, lo, hi], axis=0)
 
+    hi, mid, lo = split3(inverse)
+    inverse_split = jnp.concatenate([hi, hi, mid, mid, hi, lo], axis=1)
+
     all_e = all_of(e_rx.at[pl.ds(0, 7)], e_send, e_recv)
     all_e.wait_recv()
     total = e_rx[0]
@@ -244,13 +300,17 @@
     all_g = all_of(q_full.at[pl.ds(0, 3)], g_send, g_recv)
     all_g.wait_recv()
     q_sum = q_full[...].reshape(RANK, WIDE)
-    q_new = jnp.dot(inverse, q_sum, precision=HIGHEST, preferred_element_type=F32) * (1.0 / 32.0)
+    hi, mid, lo = split3(q_sum)
+    q_stack = jnp.concatenate([hi, mid, hi, mid, lo, hi], axis=0)
+    q_new = jnp.dot(inverse_split, q_stack, preferred_element_type=F32) * (1.0 / 32.0)
     q_out[...] = q_new[:, 0:COLS]
     core_copy.wait_send()
     all_a.wait_send()
     all_b.wait_send()
     all_c.wait_send()
     half_copy.wait_send()
+    for i in range(STEPS // 2):
+        swap(i).wait_send()
     all_d.wait_send()
     all_e.wait_send()
     all_g.wait_send()
@@ -313,6 +373,13 @@
             pltpu.VMEM(strip, F32),
             pltpu.VMEM((8,) + strip, F32),
             pltpu.VMEM((4,) + strip, F32),
+            pltpu.VMEM((COLS, ROWS // 2), F32),
+            pltpu.VMEM((COLS, ROWS // 2), F32),
+            pltpu.VMEM((COLS, ROWS // 2), BF16),
+            pltpu.VMEM((COLS, ROWS // 2), BF16),
+            pltpu.SemaphoreType.REGULAR,
+            dma((STEPS // 2,)),
+            dma((STEPS // 2,)),
             dma,
             dma((2, STEPS)),
         ]

time: 55 us -> 50.6 us (0.920)
  Pallas kernels: 54.2 us -> 49.8 us
    pallas_call x1, Pallas kernels: 52.4 us -> 48 us  [body(): pl.pallas_call(kernel, name='factors', out_shape=(jax.ShapeDtypeStruct((C...]
where the time goes in v2:
time: 50.6 us; the launch traced here: 50.4 us
  Pallas kernels  49.8 us (98%)
  between operations  0.64 us (1%)
    pallas_call x1, Pallas kernels, body(): pl.pallas_call(kernel, name='factors', out_shape=(jax.ShapeDtypeStruct((C...  48 us
    pallas_call x1, Pallas kernels, body(): pl.pallas_call(update_kernel, name='update', out_shape=(jax.ShapeDtypeStr...  1.77 us

profile of v2, /device:TPU:1, one launch (start us, length us, event | category | flops | bytes accessed | tf_op | source)
XLA Modules:
  0.0 50.4 jit_solution(15388008255328443850)
XLA Ops:
  0.6 48.0 %factors.1 = (bf16[352,2048]{1,0:T(8,128)(2,1)S(1)}, bf16[192,2048]{1,0:T(8,128)(2,1)S(1)}, f32[32,2048]{1,0:T(8,128)S(1)}, f32[32,352]{1,0:T(8,128)S(1)}) custom-call(bf16[352,2048]{1,0:T(8,128)(2,1)} %bitcast.12, bf16[352,2048]{1,0:T(8,128)(2,1)} %bitcast.13, f32[32,352]{1,0:T(8,128)} %bitcast.14), custom_call_target="tpu_custom_call" | custom-call | tf_op jit(solution)/shard_map/factors/pallas_call | solution.py:348
  48.7 1.8 %update.1 = (bf16[352,2048]{1,0:T(8,128)(2,1)}, f32[32,2048]{1,0:T(8,128)}, f32[32,352]{1,0:T(8,128)}) custom-call(bf16[352,2048]{1,0:T(8,128)(2,1)S(1)} %get-tuple-element.10.merged, bf16[192,2048]{1,0:T(8,128)(2,1)S(1)} %get-tuple-element.11.p_split, f32[32,2048]{1,0:T(8,128)S(1)} %get-tuple-element.12.p_hat, f32[32,352]{1,0:T(8,128)S(1)} %get-tuple-element.13.q_new), custom_call_target="tpu_custom_call" | custom-call | tf_op jit(solution)/shard_map/update/pallas_call | solution.py:391

commit v3 on v2

--- a/solution.py
+++ b/solution.py
@@ -83,7 +83,7 @@
 
     q_copy = pltpu.make_async_copy(q_start, q_in, q_sem)
     q_copy.start()
-    for i in range(STEPS):
+    for i in range(2):
         for copy in load(i):
             copy.start()
 
@@ -99,6 +99,9 @@
     pl.semaphore_signal(barrier, inc=1, device_id=across, device_id_type=MESH)
     pl.semaphore_signal(barrier, inc=1, device_id=sibling, device_id_type=MESH)
 
+    for i in range(2, STEPS):
+        for copy in load(i):
+            copy.start()
     q_copy.wait()
     q_narrow = q_in[...].astype(BF16)
 
@@ -198,34 +201,41 @@
     for k in range(1, 8):
         total = total + b_rx[k]
     p_full[core * 32 + mine] = total
+    batch = lax.div(mine, 8)
 
     for n, o in enumerate(OFFSETS):
         pltpu.make_async_remote_copy(
             src_ref=p_full.at[core * 32 + mine], dst_ref=p_full.at[core * 32 + mine],
-            send_sem=c_send, recv_sem=c_recv, device_id=plane_peer(o)[0], device_id_type=MESH,
-        ).start()
-    all_c = all_of(p_full.at[pl.ds(0, 31)], c_send, c_recv)
-    all_c.wait_recv()
+            send_sem=c_send, recv_sem=c_recv.at[batch], device_id=plane_peer(o)[0], device_id_type=MESH,
+        ).start()
+    def left_parts(at):
+        tiles = [p_full[pl.ds(at * 8 + h * 4, 4)].reshape(RANK, 128) for h in range(2)]
+        parts = jnp.concatenate(split3(jnp.concatenate(tiles, axis=1)), axis=0)
+        parts_buf[:, cols(at)] = parts
+        return parts
+
+    turned = (((1,), (1,)), ((), ()))
+    acc = jnp.zeros((3 * RANK, COLS), F32)
+    for i in range(STEPS // 2):
+        this = lax.rem(member * 2 + i, 4)
+
+        @pl.when(batch == this)
+        def _():
+            all_of(p_full.at[pl.ds(0, 7)], c_send, c_recv.at[this]).wait_recv()
+
+        @pl.when(batch != this)
+        def _():
+            all_of(p_full.at[pl.ds(0, 8)], c_send, c_recv.at[this]).wait_recv()
+
+        parts = left_parts(core * (STEPS // 2) + this)
+        acc = acc + lax.dot_general(parts, m_lo[:, cols(this)], turned, preferred_element_type=F32)
+        acc = acc + lax.dot_general(parts, m_hi[:, cols(this)], turned, preferred_element_type=F32)
     half = pl.ds(core * 32, 32)
     half_copy = pltpu.make_async_remote_copy(
         src_ref=p_full.at[half], dst_ref=p_full.at[half],
         send_sem=f_send, recv_sem=f_recv, device_id=sibling, device_id_type=MESH,
     )
     half_copy.start()
-
-    def left_parts(at):
-        tiles = [p_full[pl.ds(at * 8 + h * 4, 4)].reshape(RANK, 128) for h in range(2)]
-        parts = jnp.concatenate(split3(jnp.concatenate(tiles, axis=1)), axis=0)
-        parts_buf[:, cols(at)] = parts
-        return parts
-
-    turned = (((1,), (1,)), ((), ()))
-    acc = jnp.zeros((3 * RANK, COLS), F32)
-    for i in range(STEPS // 2):
-        part = slice(i * STEP, (i + 1) * STEP)
-        parts = left_parts(core * (STEPS // 2) + i)
-        acc = acc + lax.dot_general(parts, m_lo[:, part], turned, preferred_element_type=F32)
-        acc = acc + lax.dot_general(parts, m_hi[:, part], turned, preferred_element_type=F32)
     acc = acc[2 * RANK :] + acc[RANK : 2 * RANK] + acc[0:RANK]
     q_part[:, :, 0:COLS] = acc.reshape(4, 8, COLS)
     q_part[:, :, COLS:] = jnp.zeros((4, 8, WIDE - COLS), F32)
@@ -280,8 +290,8 @@
         tiles = [p_full[pl.ds(i * 8 + h * 4, 4)].reshape(RANK, 128) for h in range(2)]
         p_hat = jnp.dot(inverse, jnp.concatenate(tiles, axis=1), precision=HIGHEST, preferred_element_type=F32)
         p_out[:, cols(i)] = p_hat
-        hi, mid, lo = split3(p_hat)
-        p_split[:, cols(i)] = jnp.concatenate([hi, mid, hi, mid, lo, hi], axis=0)
+        hi, mid, _ = split3(p_hat)
+        p_split[:, cols(i)] = jnp.concatenate([hi, hi, mid], axis=0)
 
     hi, mid, lo = split3(inverse)
     inverse_split = jnp.concatenate([hi, hi, mid, mid, hi, lo], axis=1)
@@ -307,7 +317,7 @@
     core_copy.wait_send()
     all_a.wait_send()
     all_b.wait_send()
-    all_c.wait_send()
+    all_of(p_full.at[pl.ds(0, 31)], c_send, c_recv.at[0]).wait_send()
     half_copy.wait_send()
     for i in range(STEPS // 2):
         swap(i).wait_send()
@@ -321,8 +331,8 @@
     q_copy = pltpu.make_async_copy(q_new, q_out, side_sem.at[1])
     p_copy.start()
     q_copy.start()
-    hi, mid, lo = split3(q_new[...].T)
-    q_split = jnp.concatenate([hi, hi, mid, mid, hi, lo], axis=1)
+    hi, mid, _ = split3(q_new[...].T)
+    q_split = jnp.concatenate([hi, mid, hi], axis=1)
 
     def store(i):
         at = pl.ds(i * STEP, STEP)
@@ -350,7 +360,7 @@
         name="factors",
         out_shape=(
             jax.ShapeDtypeStruct((COLS, ROWS), BF16),
-            jax.ShapeDtypeStruct((6 * RANK, ROWS), BF16),
+            jax.ShapeDtypeStruct((3 * RANK, ROWS), BF16),
             jax.ShapeDtypeStruct((RANK, ROWS), F32),
             jax.ShapeDtypeStruct((RANK, COLS), F32),
         ),
@@ -383,7 +393,9 @@
             dma,
             dma((2, STEPS)),
         ]
-        + [dma] * 16,
+        + [dma] * 7
+        + [dma((4,))]
+        + [dma] * 8,
         compiler_params=pltpu.CompilerParams(
             collective_id=0, has_side_effects=True, vmem_limit_bytes=32 * 1024 * 1024
         ),

time: 50.6 us -> 50.2 us (level)
  no operation moved by 1% of the time
where the time goes in v3:
time: 50.2 us; the launch traced here: 50.1 us
  Pallas kernels  49.4 us (98%)
  between operations  0.64 us (1%)
    pallas_call x1, Pallas kernels, body(): pl.pallas_call(kernel, name='factors', out_shape=(jax.ShapeDtypeStruct((C...  47.6 us
    pallas_call x1, Pallas kernels, body(): pl.pallas_call(update_kernel, name='update', out_shape=(jax.ShapeDtypeStr...  1.84 us

profile of v3, /device:TPU:1, one launch (start us, length us, event | category | flops | bytes accessed | tf_op | source)
XLA Modules:
  0.0 50.1 jit_solution(1107201806795562027)
XLA Ops:
  0.6 47.6 %factors.1 = (bf16[352,2048]{1,0:T(8,128)(2,1)S(1)}, bf16[96,2048]{1,0:T(8,128)(2,1)S(1)}, f32[32,2048]{1,0:T(8,128)S(1)}, f32[32,352]{1,0:T(8,128)S(1)}) custom-call(bf16[352,2048]{1,0:T(8,128)(2,1)} %bitcast.12, bf16[352,2048]{1,0:T(8,128)(2,1)} %bitcast.13, f32[32,352]{1,0:T(8,128)} %bitcast.14), custom_call_target="tpu_custom_call" | custom-call | tf_op jit(solution)/shard_map/factors/pallas_call | solution.py:358
  48.2 1.8 %update.1 = (bf16[352,2048]{1,0:T(8,128)(2,1)}, f32[32,2048]{1,0:T(8,128)}, f32[32,352]{1,0:T(8,128)}) custom-call(bf16[352,2048]{1,0:T(8,128)(2,1)S(1)} %get-tuple-element.10.merged, bf16[96,2048]{1,0:T(8,128)(2,1)S(1)} %get-tuple-element.11.p_split, f32[32,2048]{1,0:T(8,128)S(1)} %get-tuple-element.12.p_hat, f32[32,352]{1,0:T(8,128)S(1)} %get-tuple-element.13.q_new), custom_call_target="tpu_custom_call" | custom-call | tf_op jit(solution)/shard_map/update/pallas_call | solution.py:403

commit v4 on v3

--- a/solution.py
+++ b/solution.py
@@ -17,6 +17,7 @@
 WIDE = 384
 STEP = 256
 STEPS = ROWS // STEP
+STRIDE = 512
 
 FAR = {0: 0, 1: 1, 2: 2, 3: 1}
 OFFSETS = sorted(
@@ -115,7 +116,7 @@
         for h in range(2):
             pt[pl.ds(at * 8 + h * 4, 4)] = part[:, h * 128 : (h + 1) * 128].reshape(4, 8, 128)
 
-    for i in range(STEPS // 2):
+    for i in range(STEPS):
         left(i)
     pl.semaphore_wait(barrier, len(OFFSETS) + 2 + group)
     for a in range(8):
@@ -129,8 +130,8 @@
         send_sem=core_send, recv_sem=core_recv, device_id=sibling, device_id_type=MESH,
     )
     core_copy.start()
-    for i in range(STEPS // 2, STEPS):
-        left(i)
+    for i in range(STEPS // 2):
+        m_src[:, i * STEP : (i + 1) * STEP] = merged_out[:, cols(half_at(i))].astype(F32)
     core_copy.wait_recv()
     a_src[...] = pt[pl.ds(core * 32, 32)] + core_rx[...]
 
@@ -149,7 +150,6 @@
         )
 
     for i in range(STEPS // 2):
-        m_src[:, i * STEP : (i + 1) * STEP] = merged_out[:, cols(half_at(i))].astype(F32)
         swap(i).start()
 
     def all_of(ref, send, recv):
@@ -335,17 +335,17 @@
     q_split = jnp.concatenate([hi, mid, hi], axis=1)
 
     def store(i):
-        at = pl.ds(i * STEP, STEP)
+        at = pl.ds(i * STRIDE, STRIDE)
         return pltpu.make_async_copy(stage.at[:, at], new_errors.at[:, at], out_sem.at[i])
 
-    for i in range(STEPS):
-        at = pl.ds(i * STEP, STEP)
+    for i in range(ROWS // STRIDE):
+        at = pl.ds(i * STRIDE, STRIDE)
         delta = jnp.dot(q_split, p_split[:, at], preferred_element_type=F32)
         stage[:, at] = (merged[:, at].astype(F32) - delta).astype(BF16)
         store(i).start()
     p_copy.wait()
     q_copy.wait()
-    for i in range(STEPS):
+    for i in range(ROWS // STRIDE):
         store(i).wait()
 
 
@@ -410,7 +410,7 @@
         ),
         in_specs=[vmem_spec] * 4,
         out_specs=(hbm_spec,) * 3,
-        scratch_shapes=[pltpu.VMEM((COLS, ROWS), BF16), dma((STEPS,)), dma((2,))],
+        scratch_shapes=[pltpu.VMEM((COLS, ROWS), BF16), dma((ROWS // STRIDE,)), dma((2,))],
         compiler_params=pltpu.CompilerParams(vmem_limit_bytes=16 * 1024 * 1024),
     )(merged, p_split, p_hat, q_new)
     return new_errors.T[None], p_hat.T, q_new.T

time: 50.2 us -> 49.6 us (0.988)
  Pallas kernels: 49.4 us -> 48.8 us
where the time goes in v4:
time: 49.6 us; the launch traced here: 49.5 us
  Pallas kernels  48.8 us (98%)
  between operations  0.64 us (1%)
    pallas_call x1, Pallas kernels, body(): pl.pallas_call(kernel, name='factors', out_shape=(jax.ShapeDtypeStruct((C...  47.2 us
    pallas_call x1, Pallas kernels, body(): pl.pallas_call(update_kernel, name='update', out_shape=(jax.ShapeDtypeStr...  1.69 us

profile of v4, /device:TPU:1, one launch (start us, length us, event | category | flops | bytes accessed | tf_op | source)
XLA Modules:
  0.0 49.5 jit_solution(11831080233512652041)
XLA Ops:
  0.6 47.2 %factors.1 = (bf16[352,2048]{1,0:T(8,128)(2,1)S(1)}, bf16[96,2048]{1,0:T(8,128)(2,1)S(1)}, f32[32,2048]{1,0:T(8,128)S(1)}, f32[32,352]{1,0:T(8,128)S(1)}) custom-call(bf16[352,2048]{1,0:T(8,128)(2,1)} %bitcast.12, bf16[352,2048]{1,0:T(8,128)(2,1)} %bitcast.13, f32[32,352]{1,0:T(8,128)} %bitcast.14), custom_call_target="tpu_custom_call" | custom-call | tf_op jit(solution)/shard_map/factors/pallas_call | solution.py:358
  47.8 1.7 %update.1 = (bf16[352,2048]{1,0:T(8,128)(2,1)}, f32[32,2048]{1,0:T(8,128)}, f32[32,352]{1,0:T(8,128)}) custom-call(bf16[352,2048]{1,0:T(8,128)(2,1)S(1)} %get-tuple-element.10.merged, bf16[96,2048]{1,0:T(8,128)(2,1)S(1)} %get-tuple-element.11.p_split, f32[32,2048]{1,0:T(8,128)S(1)} %get-tuple-element.12.p_hat, f32[32,352]{1,0:T(8,128)S(1)} %get-tuple-element.13.q_new), custom_call_target="tpu_custom_call" | custom-call | tf_op jit(solution)/shard_map/update/pallas_call | solution.py:403

commit v5 on v4

--- a/solution.py
+++ b/solution.py
@@ -125,22 +125,33 @@
         def _():
             pl.semaphore_signal(ready, inc=1, device_id=group_at(a), device_id_type=MESH)
 
-    core_copy = pltpu.make_async_remote_copy(
-        src_ref=pt.at[pl.ds(other * 32, 32)], dst_ref=core_rx,
-        send_sem=core_send, recv_sem=core_recv, device_id=sibling, device_id_type=MESH,
-    )
-    core_copy.start()
+    core_copies = [
+        pltpu.make_async_remote_copy(
+            src_ref=pt.at[pl.ds(other * 32 + m * 16, 16)], dst_ref=core_rx.at[pl.ds(m * 16, 16)],
+            send_sem=core_send.at[n], recv_sem=core_recv.at[n], device_id=sibling, device_id_type=MESH,
+        )
+        for n, m in enumerate((members[1], members[0]))
+    ]
+    for copy in core_copies:
+        copy.start()
     for i in range(STEPS // 2):
         m_src[:, i * STEP : (i + 1) * STEP] = merged_out[:, cols(half_at(i))].astype(F32)
-    core_copy.wait_recv()
-    a_src[...] = pt[pl.ds(core * 32, 32)] + core_rx[...]
-
-    for n, o in enumerate(OFFSETS):
-        device, chunk = plane_peer(o)
+
+    def send(n):
+        device, chunk = plane_peer(OFFSETS[n])
         pltpu.make_async_remote_copy(
             src_ref=a_src.at[chunk], dst_ref=a_rx.at[n],
             send_sem=a_send, recv_sem=a_recv, device_id=device, device_id_type=MESH,
         ).start()
+
+    first = [n for n, o in enumerate(OFFSETS) if o[0] == 1 and FAR[o[1]] + FAR[o[2]] >= 3]
+    rest = [n for n in range(len(OFFSETS)) if n not in first]
+    for copy, m, which in zip(core_copies, (members[1], members[0]), (first, rest)):
+        copy.wait_recv()
+        part = pl.ds(m * 16, 16)
+        a_src[part] = pt[pl.ds(core * 32 + m * 16, 16)] + core_rx[part]
+        for n in which:
+            send(n)
 
     def swap(i):
         part = pl.ds(i * STEP, STEP)
@@ -314,7 +325,8 @@
     q_stack = jnp.concatenate([hi, mid, hi, mid, lo, hi], axis=0)
     q_new = jnp.dot(inverse_split, q_stack, preferred_element_type=F32) * (1.0 / 32.0)
     q_out[...] = q_new[:, 0:COLS]
-    core_copy.wait_send()
+    for copy in core_copies:
+        copy.wait_send()
     all_a.wait_send()
     all_b.wait_send()
     all_of(p_full.at[pl.ds(0, 31)], c_send, c_recv.at[0]).wait_send()
@@ -393,7 +405,8 @@
             dma,
             dma((2, STEPS)),
         ]
-        + [dma] * 7
+        + [dma((2,))] * 2
+        + [dma] * 5
         + [dma((4,))]
         + [dma] * 8,
         compiler_params=pltpu.CompilerParams(

time: 49.6 us -> 49.6 us (level)
  no operation moved by 1% of the time
where the time goes in v5:
time: 49.6 us; the launch traced here: 49.4 us
  Pallas kernels  48.8 us (98%)
  between operations  0.64 us (1%)
    pallas_call x1, Pallas kernels, body(): pl.pallas_call(kernel, name='factors', out_shape=(jax.ShapeDtypeStruct((C...  47.1 us
    pallas_call x1, Pallas kernels, body(): pl.pallas_call(update_kernel, name='update', out_shape=(jax.ShapeDtypeStr...  1.69 us

profile of v5, /device:TPU:1, one launch (start us, length us, event | category | flops | bytes accessed | tf_op | source)
XLA Modules:
  0.0 49.4 jit_solution(7453582490846125926)
XLA Ops:
  0.6 47.1 %factors.1 = (bf16[352,2048]{1,0:T(8,128)(2,1)S(1)}, bf16[96,2048]{1,0:T(8,128)(2,1)S(1)}, f32[32,2048]{1,0:T(8,128)S(1)}, f32[32,352]{1,0:T(8,128)S(1)}) custom-call(bf16[352,2048]{1,0:T(8,128)(2,1)} %bitcast.12, bf16[352,2048]{1,0:T(8,128)(2,1)} %bitcast.13, f32[32,352]{1,0:T(8,128)} %bitcast.14), custom_call_target="tpu_custom_call" | custom-call | tf_op jit(solution)/shard_map/factors/pallas_call | solution.py:370
  47.8 1.7 %update.1 = (bf16[352,2048]{1,0:T(8,128)(2,1)}, f32[32,2048]{1,0:T(8,128)}, f32[32,352]{1,0:T(8,128)}) custom-call(bf16[352,2048]{1,0:T(8,128)(2,1)S(1)} %get-tuple-element.10.merged, bf16[96,2048]{1,0:T(8,128)(2,1)S(1)} %get-tuple-element.11.p_split, f32[32,2048]{1,0:T(8,128)S(1)} %get-tuple-element.12.p_hat, f32[32,352]{1,0:T(8,128)S(1)} %get-tuple-element.13.q_new), custom_call_target="tpu_custom_call" | custom-call | tf_op jit(solution)/shard_map/update/pallas_call | solution.py:416
